TPU v7x, 128 devices: a whole 4x4x4 slice. The times are simulated.
128 devices in a mesh: rows: 16 (over y, x_lo, core), cols: 8 (over x_hi, z).
Axes of the slice: x: 4 (x_hi: 2, x_lo: 2; x = x_hi * 2 + x_lo), y: 4, z: 4, core: 2. Of those that a mesh axis runs over, the one named last changes fastest.
Arguments:
- tokens: bfloat16 [131072, 1024], P(('rows', 'cols')), may hold values from -40 to 40
- qkv_weight: bfloat16 [1024, 3072], replicated, may hold values from -0.25 to 0.25
- out_weight: bfloat16 [1024, 1024], replicated, may hold values from -0.1875 to 0.1875
- neighbours: int32 [32, 64, 9], P('rows', 'cols'), may hold values from -1 to 2047, as said below
Outputs:
- mixed: bfloat16 [131072, 1024], P(('rows', 'cols'))
Inputs may be any that keep to these rules, and one draw needn't show every extreme that they name: `neighbours`: entry k of block (i, j)'s list is the block at offset (k // 3 - 1, k % 3 - 1) from a centre block, or -1 where that block is left out; the centre is (i, j) moved inward just enough to lie one block off every edge of the grid; block (i, j) itself is never left out.
All inputs are finite; a program needn't handle non-finite values.
Results may differ from a plain program's by a relative error of at most 0.014.
Values may be sent and summed in bfloat16 or wider, within the bound.
A program may use at most 192 MiB of HBM per device.

v0:
```python
import math

import jax
import jax.numpy as jnp
from jax import lax
from jax.sharding import PartitionSpec as P

HEADS = 16
HEAD_DIM = 64
BLK = 8
NBR = 9


def with_halo(block, sides, width):
    for axis, dim in sides:
        count = lax.axis_size(axis)
        forward = [(i, i + 1) for i in range(count - 1)]
        backward = [(target, source) for source, target in forward]
        low = lax.ppermute(
            lax.slice_in_dim(block, block.shape[dim] - width, None, axis=dim), axis, forward
        )
        high = lax.ppermute(lax.slice_in_dim(block, 0, width, axis=dim), axis, backward)
        block = jnp.concatenate([low, block, high], axis=dim)
    return block


def per_device(tokens, qkv_weight, out_weight, neighbours):
    n_cols = lax.axis_size("cols")
    blk_h = neighbours.shape[0]
    blk_w = neighbours.shape[1]
    tile_h = blk_h * BLK
    tile_w = blk_w * BLK
    features = tokens.shape[1]
    per_row = tile_h // n_cols
    projected = jnp.dot(tokens, qkv_weight, preferred_element_type=jnp.float32).astype(jnp.bfloat16)
    tile_data = lax.all_to_all(
        projected.reshape(per_row, n_cols, tile_w, 3 * features),
        "cols",
        split_axis=1,
        concat_axis=0,
        tiled=True,
    )
    tile_data = tile_data.reshape(tile_h, tile_w, 3 * features)
    queries = tile_data[:, :, :features]
    keyvals = tile_data[:, :, features:]
    extended = with_halo(keyvals, (("rows", 0), ("cols", 1)), BLK)
    ext_h = blk_h + 2
    ext_w = blk_w + 2
    key_blocks = extended.reshape(ext_h, BLK, ext_w, BLK, 2 * features).transpose(0, 2, 1, 3, 4)
    key_blocks = key_blocks.reshape(ext_h * ext_w, BLK * BLK, 2 * features)
    query_blocks = queries.reshape(blk_h, BLK, blk_w, BLK, features).transpose(0, 2, 1, 3, 4)
    grid_cols = blk_w * n_cols
    row_start = lax.axis_index("rows") * blk_h
    col_start = lax.axis_index("cols") * blk_w
    present = neighbours >= 0
    clamped = jnp.where(present, neighbours, 0)
    local_index = (clamped // grid_cols - row_start + 1) * ext_w + (
        clamped % grid_cols - col_start + 1
    )
    local_index = jnp.where(present, local_index, 0)
    block_count = blk_h * blk_w
    group_size = math.gcd(8, block_count)
    steps_count = block_count // group_size
    query_groups = query_blocks.reshape(steps_count, group_size, BLK * BLK, HEADS, HEAD_DIM)
    score_scale = HEAD_DIM ** (-0.5)

    def attend(triple):
        query_set, slots_in, present_in = triple
        key_vals = key_blocks[slots_in].reshape(group_size, NBR * BLK * BLK, 2 * features)
        key_set = key_vals[:, :, :features].reshape(group_size, NBR * BLK * BLK, HEADS, HEAD_DIM)
        value_set = key_vals[:, :, features:].reshape(group_size, NBR * BLK * BLK, HEADS, HEAD_DIM)
        scores = (
            jnp.einsum("gqhd,gkhd->ghqk", query_set, key_set, preferred_element_type=jnp.float32)
            * score_scale
        )
        key_mask = jnp.repeat(present_in, BLK * BLK, axis=1)
        scores = jnp.where(key_mask[:, None, None, :], scores, -jnp.inf)
        row_top = jnp.max(scores, axis=-1, keepdims=True)
        weights = jnp.exp(scores - row_top)
        probabilities = (weights / jnp.sum(weights, axis=-1, keepdims=True)).astype(jnp.bfloat16)
        result = jnp.einsum(
            "ghqk,gkhd->gqhd", probabilities, value_set, preferred_element_type=jnp.float32
        )
        return result.astype(jnp.bfloat16).reshape(group_size, BLK * BLK, features)

    attended = lax.map(attend, (query_groups, local_index, present))
    attended = attended.reshape(blk_h, blk_w, BLK, BLK, features).transpose(0, 2, 1, 3, 4)
    tiles_out = attended.reshape(tile_h, 1, tile_w, features)
    piece_in = lax.all_to_all(tiles_out, "cols", split_axis=0, concat_axis=1, tiled=True)
    flat_rows = piece_in.reshape(-1, features)
    result = jnp.dot(flat_rows, out_weight, preferred_element_type=jnp.float32).astype(jnp.bfloat16)
    mixed_out = result.reshape(piece_in.shape[0], piece_in.shape[1], piece_in.shape[2], features)
    return mixed_out.reshape(per_row * n_cols * tile_w, features)


def solution(mesh):
    in_specs = (P(("rows", "cols"), None), P(), P(), P("rows", "cols", None))
    out_specs = P(("rows", "cols"), None)
    return jax.shard_map(
        per_device, mesh=mesh, in_specs=in_specs, out_specs=out_specs, check_vma=False
    )
```

profile of v0, /device:TPU:6, one launch (start us, length us, event | category | flops | bytes accessed | tf_op | source)
XLA Modules:
  0.0 458.5 jit_solution(12119042994665035601)
XLA Ops:
  0.0 0.0 copy-start
  0.0 1.6 copy-done
  1.6 9.6 %convolution_convert_fusion = bf16[1024,3072]{1,0:T(8,128)(2,1)S(1)} fusion(bf16[1024,1024]{1,0:T(8,128)(2,1)S(1)} %copy-done, bf16[1024,3072]{1,0:T(8,128)(2,1)} %param.7), kind=kOutput, calls=%fused_computation.21 | convolution fusion | flops 6445596672 | bytes 14680064 | tf_op jit(solution)/shard_map/dot_general | solution.py:35
  11.2 0.6 copy.35
  11.9 78.5 %all_to_all.30 = bf16[2,8,64,3072]{3,2,0,1:T(8,128)(2,1)S(1)} all-to-all(bf16[2,8,64,3072]{3,2,0,1:T(8,128)(2,1)S(1)} %copy.35), channel_id=1, replica_groups=mesh['rows'=16,'cols'=8] {'cols'}, dimensions={1} | all-to-all | bytes 12582912 | tf_op jit(solution)/shard_map/all_to_all | solution.py:36
  90.4 0.0 copy-start.2
  90.4 0.4 fusion.23
  90.8 1.9 collective-permute-start
  92.7 3.6 collective-permute-start.1
  96.4 0.4 slice.37
  96.8 0.0 copy-done.2
  96.8 0.0 copy-start.3
  96.9 0.0 copy-start.5
  96.9 25.8 %collective-permute-done = bf16[8,64,2048]{2,1,0:T(8,128)(2,1)S(1)} collective-permute-done((bf16[8,64,2048]{2,1,0:T(8,128)(2,1)S(1)}, bf16[8,64,2048]{2,1,0:T(8,128)(2,1)S(1)}, u32[]{:S(2)}, u32[]{:S(2)}) %collective-permute-start) | collective-permute-done | bytes 2097184 | tf_op jit(solution)/shard_map/ppermute | solution.py:19
  122.7 18.3 %collective-permute-done.1 = bf16[8,64,2048]{2,1,0:T(8,128)(2,1)S(1)} collective-permute-done((bf16[8,64,2048]{2,1,0:T(8,128)(2,1)S(1)}, bf16[8,64,2048]{2,1,0:T(8,128)(2,1)S(1)}, u32[]{:S(2)}, u32[]{:S(2)}) %collective-permute-start.1) | collective-permute-done | bytes 2097184 | tf_op jit(solution)/shard_map/ppermute | solution.py:22
  140.9 0.0 copy-done.3
  140.9 0.0 copy-start.4
  140.9 1.6 pad_maximum_fusion.3
  142.5 0.4 copy-done.4
  142.9 2.1 collective-permute-start.2
  145.0 7.3 %collective-permute-start.3 = (bf16[32,8,2048]{2,1,0:T(8,128)(2,1)}, bf16[32,8,2048]{2,1,0:T(8,128)(2,1)}, u32[]{:S(2)}, u32[]{:S(2)}) collective-permute-start(bf16[32,8,2048]{2,1,0:T(8,128)(2,1)} %get-tuple-element.79), channel_id=1, source_target_pairs={{1,0},{2,1},{3,2},{4,3},{5,4},{6,5},{7,6},{9,8},{10,9},{11,10},{12... | collective-permute-start | bytes 3145736 | tf_op jit(solution)/shard_map/ppermute | solution.py:22
  152.4 0.0 copy-done.5
  152.4 1.8 slice.39
  154.2 1.5 copy.51
  155.7 6.4 %reshape.77 = bf16[2,8,64,16,64]{4,3,2,1,0:T(8,128)(2,1)} reshape(bf16[2,8,8,8,1024]{4,3,2,1,0:T(8,128)(2,1)} %bitcast.74) | data formatting | bytes 4194304 | tf_op jit(solution)/shard_map/reshape | solution.py:64
  162.1 12.1 %collective-permute-done.2 = bf16[32,8,2048]{2,1,0:T(8,128)(2,1)S(1)} collective-permute-done((bf16[32,8,2048]{2,1,0:T(8,128)(2,1)}, bf16[32,8,2048]{2,1,0:T(8,128)(2,1)S(1)}, u32[]{:S(2)}, u32[]{:S(2)}) %collective-permute-start.2) | collective-permute-done | bytes 1048608 | tf_op jit(solution)/shard_map/ppermute | solution.py:19
  174.2 1.3 collective-permute-done.3
  175.5 11.1 %pad_maximum_fusion = bf16[32,80,2048]{2,1,0:T(8,128)(2,1)} fusion(bf16[32,8,2048]{2,1,0:T(8,128)(2,1)} %collective-permute-done.3, bf16[8,64,2048]{2,1,0:T(8,128)(2,1)} %copy-done.4, bf16[16,64,2048]{2,1,0:T(8,128)(2,1)} %copy-done.3, bf16[8,64,2048]{2,1,0:T(8,128)(2,1)S(1)} %collective-permute-done, bf16[32,8,2048]{2,1,0:T(8,128)(2,1)S(1)} %collective-permute-done.2), kind=kLoop, calls=%fused_computation.20 | loop fusion | flops 52428800 | bytes 20971520 | tf_op jit(solution)/shard_map/concatenate | solution.py:23
  186.6 10.1 %copy.36 = bf16[4,10,8,8,2048]{4,3,2,1,0:T(8,128)(2,1)} copy(bf16[4,10,8,8,2048]{4,3,1,2,0:T(8,128)(2,1)} %bitcast.73) | data formatting | bytes 20971520 | tf_op jit(solution)/shard_map/transpose | solution.py:49
  196.7 223.1 %while.10 = (s32[]{:T(128)}, bf16[2,8,64,1024]{3,2,1,0:T(8,128)(2,1)}, s32[2,8,9]{2,1,0:T(8,128)S(1)}, bf16[40,64,2048]{2,1,0:T(8,128)(2,1)}, pred[2,8,9]{2,1,0:...) while((s32[]{:T(128)}, bf16[2,8,64,1024]{3,2,1,0:T(8,128)(2,1)}, s32[2,8,9]{2,1,0:T(8,128)S(1)}, ...), condition=%wide.region_3.4_spmd, body=%wide.region_0.3_spmd.sunk | while | flops 1246234368 | bytes 216097264 | solution.py:86
  196.7 0.1 reshape.96
  196.8 12.2 %gather_fusion = bf16[72,64,2048]{2,1,0:T(8,128)(2,1)} fusion(bf16[40,64,2048]{2,1,0:T(8,128)(2,1)} %get-tuple-element.144, s32[1024]{0:T(1024)S(1)} %pad_clamp_fusion.2), kind=kCustom, calls=%fused_computation.clone.1 | custom fusion | bytes 37749024 | tf_op jit(solution)/shard_map/while/body/eval_jaxpr/gather | solution.py:69
  209.0 14.8 %fusion.38 = (bf16[8,576,1024]{2,1,0:T(8,128)(2,1)}, bf16[8,576,1024]{2,1,0:T(8,128)(2,1)}) fusion(bf16[8,576,2048]{2,1,0:T(8,128)(2,1)} %bitcast.65), kind=kLoop, calls=%fused_computation.45.clone.1 | loop fusion | bytes 37748736 | tf_op jit(solution)/shard_map/while/body/eval_jaxpr/slice | solution.py:70
  223.8 14.1 %copy.58 = bf16[8,576,1024]{1,2,0:T(8,128)(2,1)} copy(bf16[8,576,1024]{2,1,0:T(8,128)(2,1)} %get-tuple-element.124) | data formatting | bytes 18874368 | tf_op jit(solution)/shard_map/while
  237.9 2.0 constant_dynamic-slice_fusion.2
  239.9 13.8 %fusion.39 = f32[8,16,64,576]{3,2,1,0:T(8,128)} fusion(bf16[8,576,16,64]{1,3,2,0:T(8,128)(2,1)} %bitcast.66, bf16[1,8,64,16,64]{4,3,2,1,0:T(8,128)(2,1)S(1)} %constant_dynamic-slice_fusion.2), kind=kOutput, calls=%fused_computation.11.clone.1 | convolution fusion | flops 603979776 | bytes 29360128 | tf_op jit(solution)/shard_map/while/body/eval_jaxpr/gqhd,gkhd->ghqk/dot_general | solution.py:73
  253.7 0.1 broadcast_in_dim.51
  253.8 0.1 broadcast_in_dim.52
  253.8 24.1 %fusion.40 = (f32[8,16,64]{2,1,0:T(8,128)S(1)}, f32[8,16,64,576]{3,2,1,0:T(8,128)}) fusion(f32[8,16,64,576]{3,2,1,0:T(8,128)} %fusion.39, pred[8,576]{1,0:T(8,128)(4,1)S(1)} %broadcast_in_dim.52), kind=kOutput, calls=%fused_computation.46.clone.1 | output fusion | flops 28312128 | bytes 37786112 | tf_op jit(solution)/shard_map/while/body/eval_jaxpr/sub | solution.py:79
  278.0 14.1 %copy.57 = bf16[8,576,1024]{1,2,0:T(8,128)(2,1)} copy(bf16[8,576,1024]{2,1,0:T(8,128)(2,1)} %get-tuple-element.123) | data formatting | bytes 18874368 | tf_op jit(solution)/shard_map/while
  292.0 13.3 %fusion.41 = bf16[8,16,64,64]{3,2,1,0:T(8,128)(2,1)} fusion(bf16[8,576,16,64]{1,3,2,0:T(8,128)(2,1)} %bitcast.68, f32[8,16,64,576]{3,2,1,0:T(8,128)} %get-tuple-element.125, f32[8,16,64]{2,1,0:T(8,128)S(1)} %get-tuple-element.126), kind=kOutput, calls=%fused_computation.12.clone.1 | convolution fusion | flops 613941248 | bytes 29392896 | tf_op jit(solution)/shard_map/while/body/eval_jaxpr/ghqk,gkhd->gqhd/dot_general | solution.py:81
  305.3 1.9 copy.59
  307.2 1.0 constant_dynamic-update-slice_fusion.2
  308.3 0.1 reshape.96
  308.4 12.2 %gather_fusion = bf16[72,64,2048]{2,1,0:T(8,128)(2,1)} fusion(bf16[40,64,2048]{2,1,0:T(8,128)(2,1)} %get-tuple-element.144, s32[1024]{0:T(1024)S(1)} %pad_clamp_fusion.2), kind=kCustom, calls=%fused_computation.clone.1 | custom fusion | bytes 37749024 | tf_op jit(solution)/shard_map/while/body/eval_jaxpr/gather | solution.py:69
  320.6 14.8 %fusion.38 = (bf16[8,576,1024]{2,1,0:T(8,128)(2,1)}, bf16[8,576,1024]{2,1,0:T(8,128)(2,1)}) fusion(bf16[8,576,2048]{2,1,0:T(8,128)(2,1)} %bitcast.65), kind=kLoop, calls=%fused_computation.45.clone.1 | loop fusion | bytes 37748736 | tf_op jit(solution)/shard_map/while/body/eval_jaxpr/slice | solution.py:70
  335.4 14.1 %copy.58 = bf16[8,576,1024]{1,2,0:T(8,128)(2,1)} copy(bf16[8,576,1024]{2,1,0:T(8,128)(2,1)} %get-tuple-element.124) | data formatting | bytes 18874368 | tf_op jit(solution)/shard_map/while
  349.5 2.0 constant_dynamic-slice_fusion.2
  351.4 13.8 %fusion.39 = f32[8,16,64,576]{3,2,1,0:T(8,128)} fusion(bf16[8,576,16,64]{1,3,2,0:T(8,128)(2,1)} %bitcast.66, bf16[1,8,64,16,64]{4,3,2,1,0:T(8,128)(2,1)S(1)} %constant_dynamic-slice_fusion.2), kind=kOutput, calls=%fused_computation.11.clone.1 | convolution fusion | flops 603979776 | bytes 29360128 | tf_op jit(solution)/shard_map/while/body/eval_jaxpr/gqhd,gkhd->ghqk/dot_general | solution.py:73
  365.2 0.1 broadcast_in_dim.51
  365.3 0.1 broadcast_in_dim.52
  365.4 24.1 %fusion.40 = (f32[8,16,64]{2,1,0:T(8,128)S(1)}, f32[8,16,64,576]{3,2,1,0:T(8,128)}) fusion(f32[8,16,64,576]{3,2,1,0:T(8,128)} %fusion.39, pred[8,576]{1,0:T(8,128)(4,1)S(1)} %broadcast_in_dim.52), kind=kOutput, calls=%fused_computation.46.clone.1 | output fusion | flops 28312128 | bytes 37786112 | tf_op jit(solution)/shard_map/while/body/eval_jaxpr/sub | solution.py:79
  389.5 14.1 %copy.57 = bf16[8,576,1024]{1,2,0:T(8,128)(2,1)} copy(bf16[8,576,1024]{2,1,0:T(8,128)(2,1)} %get-tuple-element.123) | data formatting | bytes 18874368 | tf_op jit(solution)/shard_map/while
  403.6 13.3 %fusion.41 = bf16[8,16,64,64]{3,2,1,0:T(8,128)(2,1)} fusion(bf16[8,576,16,64]{1,3,2,0:T(8,128)(2,1)} %bitcast.68, f32[8,16,64,576]{3,2,1,0:T(8,128)} %get-tuple-element.125, f32[8,16,64]{2,1,0:T(8,128)S(1)} %get-tuple-element.126), kind=kOutput, calls=%fused_computation.12.clone.1 | convolution fusion | flops 613941248 | bytes 29392896 | tf_op jit(solution)/shard_map/while/body/eval_jaxpr/ghqk,gkhd->gqhd/dot_general | solution.py:81
  416.9 1.9 copy.59
  418.8 1.0 constant_dynamic-update-slice_fusion.2
  419.8 0.0 copy-start.6
  419.8 2.0 copy.40
  421.8 32.8 %all_to_all.31 = bf16[16,1,64,1024]{3,2,1,0:T(8,128)(2,1)S(1)} all-to-all(bf16[16,1,64,1024]{3,2,1,0:T(8,128)(2,1)S(1)} %bitcast.76), channel_id=1, replica_groups=mesh['rows'=16,'cols'=8] {'cols'}, dimensions={0} | all-to-all | bytes 4194304 | tf_op jit(solution)/shard_map/all_to_all | solution.py:89
  454.6 0.2 copy.42
  454.8 0.0 copy-start.1
  454.8 0.0 copy-done.6
  454.8 3.7 convolution_convert_fusion.1
  458.5 0.0 copy-done.1
  (9 shorter events, 0.1 us)
Async XLA Ops:
  0.0 1.6 copy-start
  90.4 6.5 %copy-start.2 = (bf16[2,8,64,3072]{3,2,0,1:T(8,128)(2,1)}, bf16[2,8,64,3072]{3,2,0,1:T(8,128)(2,1)S(1)}, u32[]{:S(2)}) copy-start(bf16[2,8,64,3072]{3,2,0,1:T(8,128)(2,1)S(1)} %all_to_all.30) | copy-start | bytes 18874372
  90.8 31.9 %collective-permute-start = (bf16[8,64,2048]{2,1,0:T(8,128)(2,1)S(1)}, bf16[8,64,2048]{2,1,0:T(8,128)(2,1)S(1)}, u32[]{:S(2)}, u32[]{:S(2)}) collective-permute-start(bf16[8,64,2048]{2,1,0:T(8,128)(2,1)S(1)} %get-tuple-element.80), channel_id=1, source_target_pairs={{0,8},{8,16},{16,24},{24,32},{32,40},{40,48},{48,56},{56,64},{64,7... | collective-permute-start | bytes 6291464 | tf_op jit(solution)/shard_map/ppermute | solution.py:19
  92.7 48.2 %collective-permute-start.1 = (bf16[8,64,2048]{2,1,0:T(8,128)(2,1)S(1)}, bf16[8,64,2048]{2,1,0:T(8,128)(2,1)S(1)}, u32[]{:S(2)}, u32[]{:S(2)}) collective-permute-start(bf16[8,64,2048]{2,1,0:T(8,128)(2,1)S(1)} %get-tuple-element.81), channel_id=1, source_target_pairs={{8,0},{16,8},{24,16},{32,24},{40,32},{48,40},{56,48},{64,56},{72,6... | collective-permute-start | bytes 6291464 | tf_op jit(solution)/shard_map/ppermute | solution.py:22
  96.8 44.1 %copy-start.3 = (bf16[16,64,2048]{2,1,0:T(8,128)(2,1)}, bf16[16,64,2048]{2,1,0:T(8,128)(2,1)S(1)}, u32[]{:S(2)}) copy-start(bf16[16,64,2048]{2,1,0:T(8,128)(2,1)S(1)} %slice.37) | copy-start | bytes 12582916
  96.9 55.5 %copy-start.5 = (s32[2,8,9]{2,1,0:T(8,128)S(1)}, s32[2,8,9]{2,1,0:T(8,128)}, u32[]{:S(2)}) copy-start(s32[2,8,9]{2,1,0:T(8,128)} %param.9) | copy-start | bytes 1732
  140.9 2.0 copy-start.4
  142.9 31.3 %collective-permute-start.2 = (bf16[32,8,2048]{2,1,0:T(8,128)(2,1)}, bf16[32,8,2048]{2,1,0:T(8,128)(2,1)S(1)}, u32[]{:S(2)}, u32[]{:S(2)}) collective-permute-start(bf16[32,8,2048]{2,1,0:T(8,128)(2,1)} %get-tuple-element.78), channel_id=1, source_target_pairs={{0,1},{1,2},{2,3},{3,4},{4,5},{5,6},{6,7},{8,9},{9,10},{10,11},{11... | collective-permute-start | bytes 3145736 | tf_op jit(solution)/shard_map/ppermute | solution.py:19
  145.0 30.5 %collective-permute-start.3 = (bf16[32,8,2048]{2,1,0:T(8,128)(2,1)}, bf16[32,8,2048]{2,1,0:T(8,128)(2,1)}, u32[]{:S(2)}, u32[]{:S(2)}) collective-permute-start(bf16[32,8,2048]{2,1,0:T(8,128)(2,1)} %get-tuple-element.79), channel_id=1, source_target_pairs={{1,0},{2,1},{3,2},{4,3},{5,4},{6,5},{7,6},{9,8},{10,9},{11,10},{12... | collective-permute-start | bytes 3145736 | tf_op jit(solution)/shard_map/ppermute | solution.py:22
  419.8 35.0 %copy-start.6 = (bf16[1024,1024]{1,0:T(8,128)(2,1)S(1)}, bf16[1024,1024]{1,0:T(8,128)(2,1)}, u32[]{:S(2)}) copy-start(bf16[1024,1024]{1,0:T(8,128)(2,1)} %param.8) | copy-start | bytes 6291460
  454.8 3.7 copy-start.1
where the time goes:
time: 464 us; the launch traced here: 458 us
  local copies, waits for them, and re-layouts  146 us (31%)
  blocking collectives  111 us (24%)
  matrix products  67.5 us (15%)
  other arithmetic  60.9 us (13%)
  waiting for transfers between devices  57.5 us (12%)
  starting transfers between devices  15 us (3%)
    all_to_all x1, blocking collectives, per_device(): lax.all_to_all(projected.reshape(per_row, n_cols, tile_w, 3 * features),...  78.5 us
    while x4, local copies, waits for them, and re-layouts  56.2 us
    sub x2, other arithmetic, attend(): weights = jnp.exp(scores - row_top)  48.2 us
    ppermute x2, waiting for transfers between devices, with_halo(): lax.ppermute(lax.slice_in_dim(block, block.shape[dim] - width, None, axis...  37.9 us
    all_to_all x1, blocking collectives, per_device(): lax.all_to_all(tiles_out, 'cols', split_axis=0, concat_axis=1, tiled=True)  32.8 us
    slice x2, local copies, waits for them, and re-layouts, attend(): key_vals[:, :, :features]  29.7 us
    dot_general x2, matrix products, attend(): jnp.einsum('gqhd,gkhd->ghqk', query_set, key_set, preferred_element_type=...  27.6 us
    dot_general x2, matrix products, attend(): jnp.einsum('ghqk,gkhd->gqhd', probabilities, value_set, preferred_element...  26.6 us
  transfers between devices with their start and end apart: 4, of which 4 were waited for; matrix products, arithmetic and copies ran while one was open for 2% of the time, Pallas kernels for 0%

commit v1 on v0

v1 whole, which is shorter than its diff:
```python
import functools

import jax
import jax.numpy as jnp
from jax import lax
from jax.experimental import pallas as pl
from jax.experimental.pallas import tpu as pltpu
from jax.sharding import PartitionSpec as P

MESH = pl.DeviceIdType.MESH
BF16 = jnp.bfloat16
F32 = jnp.float32
D = 1024
HEADS = 16
HEAD_DIM = 64
GROUPS = 64
TILES = 8
SCALE = HEAD_DIM**-0.5
STAGES = ((0, 4, (0, 1)), (4, 2, (2, 3)))
QUAD = 256


def kernel(
    tok, wqkv, wout, nbr, out,
    src, win, keys, vals, quer, att, mix, wqkv_v, wout_v, nb_v, nb_s,
    load_sem, in_send, in_recv, halo_send, halo_recv, nb_send, nb_recv, nb_load, out_send, out_recv,
):
    row, col = lax.axis_index("rows"), lax.axis_index("cols")
    y, x_lo, core = row // 4, (row // 2) % 2, row % 2
    x_hi, z = col // 4, col % 4
    x = 2 * x_hi + x_lo
    g, t = 2 * y + core, 8 * x_lo + col
    has_up, has_down = g > 0, g < TILES - 1

    loads = [pltpu.make_async_copy(tok.at[r], src.at[pl.ds(1, GROUPS), r], load_sem.at[r]) for r in range(2)]
    wload = pltpu.make_async_copy(wqkv, wqkv_v, load_sem.at[2])
    oload = pltpu.make_async_copy(wout, wout_v, load_sem.at[3])
    for load in loads:
        load.start()
    wload.start()
    oload.start()

    barrier = pltpu.get_barrier_semaphore()
    place = 8 * (row % 4) + col

    def greet(i, carry):
        other = (place + i) % 32
        pl.semaphore_signal(barrier, inc=1, device_id=(4 * y + other // 8, other % 8), device_id_type=MESH)
        return carry

    lax.fori_loop(1, 32, greet, 0)
    step_y = 2 * core - 1
    outer = jnp.logical_and(y + step_y >= 0, y + step_y < TILES // 2)

    @pl.when(outer)
    def _():
        pl.semaphore_signal(
            barrier, inc=1, device_id=(4 * (y + step_y) + 2 * x_lo + 1 - core, col), device_id_type=MESH
        )

    src[0] = jnp.zeros((2, 8, D), BF16)
    src[GROUPS + 1] = jnp.zeros((2, 8, D), BF16)

    @pl.when(jnp.logical_not(has_up))
    def _():
        for c in range(6):
            win[c, 0:8] = jnp.zeros((8, 8, D), BF16)

    @pl.when(jnp.logical_not(has_down))
    def _():
        for c in range(6):
            win[c, 40:48] = jnp.zeros((8, 8, D), BF16)

    for load in loads:
        load.wait()
    pl.semaphore_wait(barrier, jnp.where(outer, 32, 31))

    for e in range(2):
        there = 2 * col + e
        dest = (4 * y + 2 * x_hi + x_lo, there % 8)
        own = jnp.logical_and(dest[0] == row, dest[1] == col)

        @pl.when(own)
        def _(dest=dest):
            pltpu.make_async_copy(nbr, nb_v.at[core], nb_recv.at[core]).start()

        @pl.when(jnp.logical_not(own))
        def _(dest=dest, e=e):
            pltpu.make_async_remote_copy(
                nbr, nb_v.at[core], nb_send.at[e], nb_recv.at[core], device_id=dest, device_id_type=MESH
            ).start()

    at_row = 8 + 16 * core + 2 * col
    band = 2 * core + x_hi
    meets = core == x_lo

    for k, (first, count, _) in enumerate(STAGES):

        def send(s, carry, k=k, first=first, count=count):
            turn = (5 * s) % 16
            x2, z2 = (x + turn // 4) % 4, (z + turn) % 4
            col2 = 4 * (x2 // 2) + z2
            t2 = 8 * (x2 % 2) + col2
            source = src.at[pl.ds(4 * t2 + first, count)]
            target = win.at[pl.ds(first, count), pl.ds(at_row, 2)]
            own = jnp.logical_and(s == 0, meets)

            @pl.when(own)
            def _():
                pltpu.make_async_copy(source, target, in_recv.at[k, band]).start()

            @pl.when(jnp.logical_not(own))
            def _():
                pltpu.make_async_remote_copy(
                    source, target, in_send.at[k], in_recv.at[k, band],
                    device_id=(4 * y + 2 * (x2 % 2) + x_lo, col2), device_id_type=MESH,
                ).start()

            return carry

        lax.fori_loop(0, 16, send, 0)

    def band_wait(k, b):
        part = win.at[pl.ds(STAGES[k][0], STAGES[k][1]), pl.ds(8 + 8 * b, 8)]
        pltpu.make_async_copy(part, part, in_recv.at[k, b]).wait()

    def halo(k, down):
        first, count, _ = STAGES[k]
        g2 = g + 1 if down else g - 1
        source = win.at[pl.ds(first, count), pl.ds(32 if down else 8, 8)]
        target = win.at[pl.ds(first, count), pl.ds(0 if down else 40, 8)]
        way = 1 if down else 0
        return pltpu.make_async_remote_copy(
            source, target, halo_send.at[k, way], halo_recv.at[k, way],
            device_id=(4 * (g2 // 2) + 2 * x_lo + g2 % 2, col), device_id_type=MESH,
        )

    def arrive(k):
        band_wait(k, 0)

        @pl.when(has_up)
        def _():
            halo(k, False).start()

        band_wait(k, 3)

        @pl.when(has_down)
        def _():
            halo(k, True).start()

        band_wait(k, 1)
        band_wait(k, 2)

    def halo_wait(k):
        @pl.when(has_up)
        def _():
            halo(k, True).wait_recv()

        @pl.when(has_down)
        def _():
            halo(k, False).wait_recv()

    def project_inner(c):
        x_in = win[c, 8:40].reshape(256, D)

        def tile(n, carry):
            at = pl.multiple_of(n * 512, 512)
            kk = jnp.dot(x_in, wqkv_v[:, pl.ds(D + at, 512)], preferred_element_type=F32)
            keys[c, 64:320, pl.ds(at, 512)] = kk.astype(BF16)
            vv = jnp.dot(x_in, wqkv_v[:, pl.ds(2 * D + at, 512)], preferred_element_type=F32)
            vals[c, 64:320, pl.ds(at, 512)] = vv.astype(BF16)
            return carry

        lax.fori_loop(0, 2, tile, 0)

    def project_queries(j):
        x_in = win[j + 1, 8:40].reshape(256, D)

        def tile(n, carry):
            at = pl.multiple_of(n * 512, 512)
            qq = jnp.dot(x_in, wqkv_v[:, pl.ds(at, 512)], preferred_element_type=F32)
            quer[j, :, pl.ds(at, 512)] = (qq.astype(BF16) * SCALE).astype(BF16)
            return carry

        lax.fori_loop(0, 2, tile, 0)

    def project_halo(first, count):
        parts = []
        for c in range(first, first + count):
            parts += [win[c, 0:8].reshape(64, D), win[c, 40:48].reshape(64, D)]
        x_in = jnp.concatenate(parts, axis=0)

        def tile(n, carry):
            at = pl.multiple_of(n * 512, 512)
            kk = jnp.dot(x_in, wqkv_v[:, pl.ds(D + at, 512)], preferred_element_type=F32).astype(BF16)
            vv = jnp.dot(x_in, wqkv_v[:, pl.ds(2 * D + at, 512)], preferred_element_type=F32).astype(BF16)
            for i, c in enumerate(range(first, first + count)):
                keys[c, 0:64, pl.ds(at, 512)] = kk[128 * i : 128 * i + 64]
                keys[c, 320:384, pl.ds(at, 512)] = kk[128 * i + 64 : 128 * i + 128]
                vals[c, 0:64, pl.ds(at, 512)] = vv[128 * i : 128 * i + 64]
                vals[c, 320:384, pl.ds(at, 512)] = vv[128 * i + 64 : 128 * i + 128]
            return carry

        lax.fori_loop(0, 2, tile, 0)

    lane_head = lax.broadcasted_iota(jnp.int32, (1, QUAD), 1) // HEAD_DIM

    def attend(j):
        at_col = j
        if j == 0:
            at_col = j + jnp.where(t == 0, 1, 0)
        if j == 3:
            at_col = j - jnp.where(t == 15, 1, 0)

        def block(i, carry):
            at_blk = i + jnp.where(jnp.logical_and(g == 0, i == 0), 1, 0)
            at_blk = at_blk - jnp.where(jnp.logical_and(g == TILES - 1, i == 3), 1, 0)
            rows = pl.ds(pl.multiple_of(64 * at_blk, 64), 192)
            q_rows = pl.ds(pl.multiple_of(64 * i, 64), 64)
            key_at = lax.broadcasted_iota(jnp.int32, (1, 576), 1) // 64
            bias = jnp.zeros((1, 576), F32)
            for kc in range(3):
                for kr in range(3):
                    entry = nb_s[i // 2, i % 2, 4 * (col % 2) + j, 3 * kr + kc]
                    here = jnp.where(entry >= 0, 0.0, -jnp.inf).astype(F32)
                    bias = jnp.where(key_at == 3 * kc + kr, here, bias)
            for h in range(HEADS // 4):
                lanes = pl.ds(h * QUAD, QUAD)
                q4 = quer[j, q_rows, lanes]
                stacked = jnp.concatenate(
                    [jnp.where(lane_head == n, q4, jnp.zeros_like(q4)) for n in range(4)], axis=0
                )
                k4 = jnp.concatenate([keys[at_col + kc, rows, lanes] for kc in range(3)], axis=0)
                v4 = jnp.concatenate([vals[at_col + kc, rows, lanes] for kc in range(3)], axis=0)
                s = lax.dot_general(stacked, k4, (((1,), (1,)), ((), ())), preferred_element_type=F32)
                s = s + bias
                p = jnp.exp(s - jnp.max(s, axis=1, keepdims=True))
                total = jnp.sum(p, axis=1, keepdims=True)
                r = jnp.dot(p.astype(BF16), v4, preferred_element_type=F32) / total
                o = jnp.where(lane_head == 0, r[0:64], r[64:128])
                o = jnp.where(lane_head == 2, r[128:192], o)
                o = jnp.where(lane_head == 3, r[192:256], o)
                att[q_rows, lanes] = o.astype(BF16)
            return carry

        lax.fori_loop(0, 4, block, 0)

        def tile(n, carry):
            at = pl.multiple_of(n * 512, 512)
            mm = jnp.dot(att[...], wout_v[:, pl.ds(at, 512)], preferred_element_type=F32).astype(BF16)
            mix[j, :, :, pl.ds(at, 512)] = mm.reshape(32, 8, 512)
            return carry

        lax.fori_loop(0, 2, tile, 0)

    def send_out(k, first, count):
        def send(s, carry):
            turn = (5 * s) % 16
            z2 = (z + turn) % 4
            x_hi2 = (x_hi + turn // 8) % 2
            core2 = (core + turn // 4) % 2
            col2 = 4 * x_hi2 + z2
            pair = 8 * core2 + col2
            source = mix.at[pl.ds(first, count), pl.ds(2 * pair, 2)]
            target = out.at[pl.ds(4 * t + first, count)]
            own = jnp.logical_and(s == 0, meets)

            @pl.when(own)
            def _():
                pltpu.make_async_copy(source, target, out_recv).start()

            @pl.when(jnp.logical_not(own))
            def _():
                pltpu.make_async_remote_copy(
                    source, target, out_send.at[k], out_recv,
                    device_id=(4 * y + 2 * core + core2, col2), device_id_type=MESH,
                ).start()

            return carry

        lax.fori_loop(0, 16, send, 0)

    def lists_in():
        for b in range(2):
            part = nb_v.at[b]
            pltpu.make_async_copy(part, part, nb_recv.at[b]).wait()
        down = pltpu.make_async_copy(nb_v, nb_s, nb_load)
        down.start()
        down.wait()

    wload.wait()
    oload.wait()
    for k, (first, count, columns) in enumerate(STAGES):
        arrive(k)
        for c in range(first, first + count):
            project_inner(c)
            if 1 <= c <= 4:
                project_queries(c - 1)
        halo_wait(k)
        project_halo(first, count)
        if k == 0:
            lists_in()
        for j in columns:
            attend(j)
        send_out(k, columns[0], len(columns))

    for e in range(2):
        there = 2 * col + e
        own = jnp.logical_and(4 * y + 2 * x_hi + x_lo == row, there % 8 == col)

        @pl.when(jnp.logical_not(own))
        def _(e=e):
            pltpu.make_async_copy(nbr, nbr, nb_send.at[e]).wait()

    for k, (first, count, columns) in enumerate(STAGES):
        for number, when in ((15, meets), (16, jnp.logical_not(meets))):

            @pl.when(when)
            def _(k=k, count=count, columns=columns, number=number):
                sent = win.at[pl.ds(0, count), pl.ds(0, 2 * number)]
                pltpu.make_async_copy(sent, sent, in_send.at[k]).wait()
                mixed = mix.at[pl.ds(0, len(columns)), pl.ds(0, 2 * number)]
                pltpu.make_async_copy(mixed, mixed, out_send.at[k]).wait()

        @pl.when(has_up)
        def _(k=k):
            halo(k, False).wait_send()

        @pl.when(has_down)
        def _(k=k):
            halo(k, True).wait_send()

    pltpu.make_async_copy(out, out, out_recv).wait()


def per_device(tokens, qkv_weight, out_weight, neighbours):
    stages = len(STAGES)
    any_space = pl.BlockSpec(memory_space=pl.ANY)
    dma = pltpu.SemaphoreType.DMA
    mixed = pl.pallas_call(
        kernel,
        out_shape=jax.ShapeDtypeStruct((GROUPS, 2, 8, D), BF16),
        in_specs=[any_space] * 4,
        out_specs=any_space,
        scratch_shapes=[
            pltpu.VMEM((GROUPS + 2, 2, 8, D), BF16),
            pltpu.VMEM((6, 48, 8, D), BF16),
            pltpu.VMEM((6, 384, D), BF16),
            pltpu.VMEM((6, 384, D), BF16),
            pltpu.VMEM((4, 256, D), BF16),
            pltpu.VMEM((256, D), BF16),
            pltpu.VMEM((4, 32, 8, D), BF16),
            pltpu.VMEM((D, 3 * D), BF16),
            pltpu.VMEM((D, D), BF16),
            pltpu.VMEM((2, 2, 8, 9), jnp.int32),
            pltpu.SMEM((2, 2, 8, 9), jnp.int32),
            dma((4,)),
            dma((stages,)),
            dma((stages, 4)),
            dma((stages, 2)),
            dma((stages, 2)),
            dma((2,)),
            dma((2,)),
            dma,
            dma((stages,)),
            dma,
        ],
        compiler_params=pltpu.CompilerParams(
            collective_id=0, has_side_effects=True, vmem_limit_bytes=56 * 1024 * 1024
        ),
    )(tokens.reshape(2, GROUPS, 8, D), qkv_weight, out_weight, neighbours)
    return mixed.transpose(1, 0, 2, 3).reshape(1024, D)


def solution(mesh):
    in_specs = (P(("rows", "cols"), None), P(), P(), P("rows", "cols", None))
    out_specs = P(("rows", "cols"), None)
    return jax.shard_map(
        per_device, mesh=mesh, in_specs=in_specs, out_specs=out_specs, check_vma=False
    )
```

time: 464 us -> 98.3 us (0.21)
  local copies, waits for them, and re-layouts: 146 us -> 3.12 us
  blocking collectives: 111 us -> 0 us
  Pallas kernels: 0 us -> 93.5 us
  matrix products: 67.5 us -> 0 us
  other arithmetic: 60.9 us -> 0 us
  waiting for transfers between devices: 57.5 us -> 0 us
  starting transfers between devices: 15 us -> 0 us
    all_to_all x2 -> x0, blocking collectives: 111 us -> none  [the longest x1 78.5 us: per_device(): lax.all_to_all(projected.reshape(per_row, n_cols, tile_w, 3 * features),...]
    pallas_call x0 -> x1, Pallas kernels: none -> 93.5 us  [per_device(): pl.pallas_call(kernel, out_shape=jax.ShapeDtypeStruct((GROUPS, 2, 8, D),...]
    dot_general x6 -> x0, matrix products: 67.5 us -> none  [the longest x2 27.6 us: attend(): jnp.einsum('gqhd,gkhd->ghqk', query_set, key_set, preferred_element_type=...]
    ppermute x4 -> x0, waiting for transfers between devices: 57.5 us -> none  [the longest x2 37.9 us: with_halo(): lax.ppermute(lax.slice_in_dim(block, block.shape[dim] - width, None, axis...]
    while x4 -> x0, local copies, waits for them, and re-layouts: 56.2 us -> none
    sub x2 -> x0, other arithmetic: 48.2 us -> none  [attend(): weights = jnp.exp(scores - row_top)]
    slice x5 -> x0, local copies, waits for them, and re-layouts: 32.3 us -> none  [the longest x2 29.7 us: attend(): key_vals[:, :, :features]]
    gather x2 -> x0, local copies, waits for them, and re-layouts: 24.4 us -> none  [attend(): key_blocks[slots_in].reshape(group_size, NBR * BLK * BLK, 2 * features)]
  transfers between devices with their start and end apart: 4 -> 0, of which waited for: 4 -> 0; matrix products, arithmetic and copies ran while one was open for 2% -> 0% of each run, Pallas kernels for 0% -> 0%
where the time goes in v1:
time: 98.3 us; the launch traced here: 96.7 us
  Pallas kernels  93.5 us (95%)
  local copies, waits for them, and re-layouts  3.12 us (3%)
    pallas_call x1, Pallas kernels, per_device(): pl.pallas_call(kernel, out_shape=jax.ShapeDtypeStruct((GROUPS, 2, 8, D),...  93.5 us
    transpose x1, local copies, waits for them, and re-layouts, per_device(): return mixed.transpose(1, 0, 2, 3).reshape(1024, D)  3.12 us

profile of v1, /device:TPU:6, one launch (start us, length us, event | category | flops | bytes accessed | tf_op | source)
XLA Modules:
  0.0 96.7 jit_solution(8724050553934689035)
XLA Ops:
  0.0 93.5 %shard_map.46 = bf16[64,2,8,1024]{3,2,1,0:T(8,128)(2,1)} custom-call(bf16[2,64,8,1024]{3,2,1,0:T(8,128)(2,1)} %bitcast.4, bf16[1024,3072]{1,0:T(8,128)(2,1)} %wqkv.1, bf16[1024,1024]{1,0:T(8,128)(2,1)} %wout.1, s32[2,8,9]{2,1,0:T(8,128)} %nbr.1), custom_call_target="tpu_custom_call" | custom-call | tf_op jit(solution)/shard_map/pallas_call | solution.py:340
  93.5 3.1 %copy.5 = bf16[2,64,8,1024]{3,2,1,0:T(8,128)(2,1)} copy(bf16[2,64,8,1024]{3,2,0,1:T(8,128)(2,1)} %bitcast.3) | data formatting | bytes 4194304 | tf_op jit(solution)/shard_map/transpose | solution.py:372

commit v2 on v1

--- a/solution.py
+++ b/solution.py
@@ -16,7 +16,8 @@
 GROUPS = 64
 TILES = 8
 SCALE = HEAD_DIM**-0.5
-STAGES = ((0, 4, (0, 1)), (4, 2, (2, 3)))
+STAGES = 6
+COLS = 4
 QUAD = 256
 
 
@@ -94,41 +95,46 @@
     band = 2 * core + x_hi
     meets = core == x_lo
 
-    for k, (first, count, _) in enumerate(STAGES):
-
-        def send(s, carry, k=k, first=first, count=count):
-            turn = (5 * s) % 16
-            x2, z2 = (x + turn // 4) % 4, (z + turn) % 4
-            col2 = 4 * (x2 // 2) + z2
-            t2 = 8 * (x2 % 2) + col2
-            source = src.at[pl.ds(4 * t2 + first, count)]
-            target = win.at[pl.ds(first, count), pl.ds(at_row, 2)]
-            own = jnp.logical_and(s == 0, meets)
-
-            @pl.when(own)
-            def _():
-                pltpu.make_async_copy(source, target, in_recv.at[k, band]).start()
-
-            @pl.when(jnp.logical_not(own))
-            def _():
-                pltpu.make_async_remote_copy(
-                    source, target, in_send.at[k], in_recv.at[k, band],
-                    device_id=(4 * y + 2 * (x2 % 2) + x_lo, col2), device_id_type=MESH,
-                ).start()
-
-            return carry
-
-        lax.fori_loop(0, 16, send, 0)
+    shift = jnp.where(t == 0, 1, 0)
+
+    def place_of(k):
+        return (k + shift) % 6
+
+    def send_in(n, carry):
+        k, s = n // 16, n % 16
+        turn = (5 * s) % 16
+        x2, z2 = (x + turn // 4) % 4, (z + turn) % 4
+        col2 = 4 * (x2 // 2) + z2
+        t2 = 8 * (x2 % 2) + col2
+        c2 = (k + jnp.where(t2 == 0, 1, 0)) % 6
+        source = src.at[4 * t2 + c2]
+        target = win.at[c2, pl.ds(at_row, 2)]
+        own = jnp.logical_and(s == 0, meets)
+
+        @pl.when(own)
+        def _():
+            pltpu.make_async_copy(source, target, in_recv.at[k, band]).start()
+
+        @pl.when(jnp.logical_not(own))
+        def _():
+            pltpu.make_async_remote_copy(
+                source, target, in_send, in_recv.at[k, band],
+                device_id=(4 * y + 2 * (x2 % 2) + x_lo, col2), device_id_type=MESH,
+            ).start()
+
+        return carry
+
+    lax.fori_loop(0, 16 * STAGES, send_in, 0)
 
     def band_wait(k, b):
-        part = win.at[pl.ds(STAGES[k][0], STAGES[k][1]), pl.ds(8 + 8 * b, 8)]
+        part = win.at[0, pl.ds(8 + 8 * b, 8)]
         pltpu.make_async_copy(part, part, in_recv.at[k, b]).wait()
 
     def halo(k, down):
-        first, count, _ = STAGES[k]
+        c = place_of(k)
         g2 = g + 1 if down else g - 1
-        source = win.at[pl.ds(first, count), pl.ds(32 if down else 8, 8)]
-        target = win.at[pl.ds(first, count), pl.ds(0 if down else 40, 8)]
+        source = win.at[c, pl.ds(32 if down else 8, 8)]
+        target = win.at[c, pl.ds(0 if down else 40, 8)]
         way = 1 if down else 0
         return pltpu.make_async_remote_copy(
             source, target, halo_send.at[k, way], halo_recv.at[k, way],
@@ -160,18 +166,48 @@
         def _():
             halo(k, False).wait_recv()
 
-    def project_inner(c):
-        x_in = win[c, 8:40].reshape(256, D)
-
+    def project(x_in, store):
         def tile(n, carry):
             at = pl.multiple_of(n * 512, 512)
             kk = jnp.dot(x_in, wqkv_v[:, pl.ds(D + at, 512)], preferred_element_type=F32)
-            keys[c, 64:320, pl.ds(at, 512)] = kk.astype(BF16)
             vv = jnp.dot(x_in, wqkv_v[:, pl.ds(2 * D + at, 512)], preferred_element_type=F32)
-            vals[c, 64:320, pl.ds(at, 512)] = vv.astype(BF16)
+            store(pl.ds(at, 512), kk.astype(BF16), vv.astype(BF16))
             return carry
 
         lax.fori_loop(0, 2, tile, 0)
+
+    def project_inner(k):
+        c = place_of(k)
+
+        def store(lanes, kk, vv):
+            keys[c, 64:320, lanes] = kk
+            vals[c, 64:320, lanes] = vv
+
+        project(win[c, 8:40].reshape(256, D), store)
+
+    def project_whole(k):
+        c = place_of(k)
+
+        def store(lanes, kk, vv):
+            keys[c, :, lanes] = kk
+            vals[c, :, lanes] = vv
+
+        project(win[c].reshape(384, D), store)
+
+    def project_halo(ks):
+        places = [place_of(k) for k in ks]
+
+        def store(lanes, kk, vv):
+            for i, c in enumerate(places):
+                keys[c, 0:64, lanes] = kk[128 * i : 128 * i + 64]
+                keys[c, 320:384, lanes] = kk[128 * i + 64 : 128 * i + 128]
+                vals[c, 0:64, lanes] = vv[128 * i : 128 * i + 64]
+                vals[c, 320:384, lanes] = vv[128 * i + 64 : 128 * i + 128]
+
+        parts = []
+        for c in places:
+            parts += [win[c, 0:8].reshape(64, D), win[c, 40:48].reshape(64, D)]
+        project(jnp.concatenate(parts, axis=0), store)
 
     def project_queries(j):
         x_in = win[j + 1, 8:40].reshape(256, D)
@@ -179,40 +215,23 @@
         def tile(n, carry):
             at = pl.multiple_of(n * 512, 512)
             qq = jnp.dot(x_in, wqkv_v[:, pl.ds(at, 512)], preferred_element_type=F32)
-            quer[j, :, pl.ds(at, 512)] = (qq.astype(BF16) * SCALE).astype(BF16)
+            quer[:, pl.ds(at, 512)] = (qq.astype(BF16) * SCALE).astype(BF16)
             return carry
 
         lax.fori_loop(0, 2, tile, 0)
 
-    def project_halo(first, count):
-        parts = []
-        for c in range(first, first + count):
-            parts += [win[c, 0:8].reshape(64, D), win[c, 40:48].reshape(64, D)]
-        x_in = jnp.concatenate(parts, axis=0)
-
-        def tile(n, carry):
-            at = pl.multiple_of(n * 512, 512)
-            kk = jnp.dot(x_in, wqkv_v[:, pl.ds(D + at, 512)], preferred_element_type=F32).astype(BF16)
-            vv = jnp.dot(x_in, wqkv_v[:, pl.ds(2 * D + at, 512)], preferred_element_type=F32).astype(BF16)
-            for i, c in enumerate(range(first, first + count)):
-                keys[c, 0:64, pl.ds(at, 512)] = kk[128 * i : 128 * i + 64]
-                keys[c, 320:384, pl.ds(at, 512)] = kk[128 * i + 64 : 128 * i + 128]
-                vals[c, 0:64, pl.ds(at, 512)] = vv[128 * i : 128 * i + 64]
-                vals[c, 320:384, pl.ds(at, 512)] = vv[128 * i + 64 : 128 * i + 128]
-            return carry
-
-        lax.fori_loop(0, 2, tile, 0)
-
     lane_head = lax.broadcasted_iota(jnp.int32, (1, QUAD), 1) // HEAD_DIM
 
-    def attend(j):
+    def attend(j, between):
         at_col = j
         if j == 0:
-            at_col = j + jnp.where(t == 0, 1, 0)
+            at_col = j + shift
         if j == 3:
             at_col = j - jnp.where(t == 15, 1, 0)
 
         def block(i, carry):
+            if between is not None:
+                pl.when(i == 2)(between)
             at_blk = i + jnp.where(jnp.logical_and(g == 0, i == 0), 1, 0)
             at_blk = at_blk - jnp.where(jnp.logical_and(g == TILES - 1, i == 3), 1, 0)
             rows = pl.ds(pl.multiple_of(64 * at_blk, 64), 192)
@@ -226,7 +245,7 @@
                     bias = jnp.where(key_at == 3 * kc + kr, here, bias)
             for h in range(HEADS // 4):
                 lanes = pl.ds(h * QUAD, QUAD)
-                q4 = quer[j, q_rows, lanes]
+                q4 = quer[q_rows, lanes]
                 stacked = jnp.concatenate(
                     [jnp.where(lane_head == n, q4, jnp.zeros_like(q4)) for n in range(4)], axis=0
                 )
@@ -253,7 +272,7 @@
 
         lax.fori_loop(0, 2, tile, 0)
 
-    def send_out(k, first, count):
+    def send_out(j):
         def send(s, carry):
             turn = (5 * s) % 16
             z2 = (z + turn) % 4
@@ -261,8 +280,8 @@
             core2 = (core + turn // 4) % 2
             col2 = 4 * x_hi2 + z2
             pair = 8 * core2 + col2
-            source = mix.at[pl.ds(first, count), pl.ds(2 * pair, 2)]
-            target = out.at[pl.ds(4 * t + first, count)]
+            source = mix.at[j, pl.ds(2 * pair, 2)]
+            target = out.at[4 * t + j]
             own = jnp.logical_and(s == 0, meets)
 
             @pl.when(own)
@@ -272,7 +291,7 @@
             @pl.when(jnp.logical_not(own))
             def _():
                 pltpu.make_async_remote_copy(
-                    source, target, out_send.at[k], out_recv,
+                    source, target, out_send, out_recv,
                     device_id=(4 * y + 2 * core + core2, col2), device_id_type=MESH,
                 ).start()
 
@@ -290,19 +309,21 @@
 
     wload.wait()
     oload.wait()
-    for k, (first, count, columns) in enumerate(STAGES):
+    for k in range(3):
         arrive(k)
-        for c in range(first, first + count):
-            project_inner(c)
-            if 1 <= c <= 4:
-                project_queries(c - 1)
+        project_inner(k)
+    project_queries(0)
+    lists_in()
+    for k in range(3):
         halo_wait(k)
-        project_halo(first, count)
-        if k == 0:
-            lists_in()
-        for j in columns:
-            attend(j)
-        send_out(k, columns[0], len(columns))
+    project_halo(range(3))
+    for j in range(COLS):
+        if j > 0:
+            project_queries(j)
+            halo_wait(j + 2)
+            project_whole(j + 2)
+        attend(j, functools.partial(arrive, j + 3) if j + 3 < STAGES else None)
+        send_out(j)
 
     for e in range(2):
         there = 2 * col + e
@@ -312,15 +333,16 @@
         def _(e=e):
             pltpu.make_async_copy(nbr, nbr, nb_send.at[e]).wait()
 
-    for k, (first, count, columns) in enumerate(STAGES):
-        for number, when in ((15, meets), (16, jnp.logical_not(meets))):
-
-            @pl.when(when)
-            def _(k=k, count=count, columns=columns, number=number):
-                sent = win.at[pl.ds(0, count), pl.ds(0, 2 * number)]
-                pltpu.make_async_copy(sent, sent, in_send.at[k]).wait()
-                mixed = mix.at[pl.ds(0, len(columns)), pl.ds(0, 2 * number)]
-                pltpu.make_async_copy(mixed, mixed, out_send.at[k]).wait()
+    for number, when in ((15, meets), (16, jnp.logical_not(meets))):
+
+        @pl.when(when)
+        def _(number=number):
+            sent = win.at[:, pl.ds(0, 2 * number)]
+            pltpu.make_async_copy(sent, sent, in_send).wait()
+            mixed = mix.at[:, pl.ds(0, 2 * number)]
+            pltpu.make_async_copy(mixed, mixed, out_send).wait()
+
+    for k in range(STAGES):
 
         @pl.when(has_up)
         def _(k=k):
@@ -334,7 +356,6 @@
 
 
 def per_device(tokens, qkv_weight, out_weight, neighbours):
-    stages = len(STAGES)
     any_space = pl.BlockSpec(memory_space=pl.ANY)
     dma = pltpu.SemaphoreType.DMA
     mixed = pl.pallas_call(
@@ -347,7 +368,7 @@
             pltpu.VMEM((6, 48, 8, D), BF16),
             pltpu.VMEM((6, 384, D), BF16),
             pltpu.VMEM((6, 384, D), BF16),
-            pltpu.VMEM((4, 256, D), BF16),
+            pltpu.VMEM((256, D), BF16),
             pltpu.VMEM((256, D), BF16),
             pltpu.VMEM((4, 32, 8, D), BF16),
             pltpu.VMEM((D, 3 * D), BF16),
@@ -355,14 +376,14 @@
             pltpu.VMEM((2, 2, 8, 9), jnp.int32),
             pltpu.SMEM((2, 2, 8, 9), jnp.int32),
             dma((4,)),
-            dma((stages,)),
-            dma((stages, 4)),
-            dma((stages, 2)),
-            dma((stages, 2)),
+            dma,
+            dma((STAGES, 4)),
+            dma((STAGES, 2)),
+            dma((STAGES, 2)),
             dma((2,)),
             dma((2,)),
             dma,
-            dma((stages,)),
+            dma,
             dma,
         ],
         compiler_params=pltpu.CompilerParams(

time: 98.3 us -> 84.1 us (0.86); the launches traced: 96.7 us -> 83.5 us
  Pallas kernels: 93.5 us -> 80.4 us
    pallas_call x1, Pallas kernels: 93.5 us -> 80.4 us  [per_device(): pl.pallas_call(kernel, out_shape=jax.ShapeDtypeStruct((GROUPS, 2, 8, D),...]
where the time goes in v2:
time: 84.1 us; the launch traced here: 83.5 us
  Pallas kernels  80.4 us (96%)
  local copies, waits for them, and re-layouts  3.12 us (4%)
    pallas_call x1, Pallas kernels, per_device(): pl.pallas_call(kernel, out_shape=jax.ShapeDtypeStruct((GROUPS, 2, 8, D),...  80.4 us
    transpose x1, local copies, waits for them, and re-layouts, per_device(): return mixed.transpose(1, 0, 2, 3).reshape(1024, D)  3.12 us

profile of v2, /device:TPU:6, one launch (start us, length us, event | category | flops | bytes accessed | tf_op | source)
XLA Modules:
  0.0 83.5 jit_solution(15827498180306838015)
XLA Ops:
  0.0 80.4 %shard_map.46 = bf16[64,2,8,1024]{3,2,1,0:T(8,128)(2,1)} custom-call(bf16[2,64,8,1024]{3,2,1,0:T(8,128)(2,1)} %bitcast.4, bf16[1024,3072]{1,0:T(8,128)(2,1)} %wqkv.1, bf16[1024,1024]{1,0:T(8,128)(2,1)} %wout.1, s32[2,8,9]{2,1,0:T(8,128)} %nbr.1), custom_call_target="tpu_custom_call" | custom-call | tf_op jit(solution)/shard_map/pallas_call | solution.py:361
  80.4 3.1 %copy.5 = bf16[2,64,8,1024]{3,2,1,0:T(8,128)(2,1)} copy(bf16[2,64,8,1024]{3,2,0,1:T(8,128)(2,1)} %bitcast.3) | data formatting | bytes 4194304 | tf_op jit(solution)/shard_map/transpose | solution.py:393

commit v3 on v2

--- a/solution.py
+++ b/solution.py
@@ -19,13 +19,18 @@
 STAGES = 6
 COLS = 4
 QUAD = 256
+QUADS = HEADS // 4
+KEYS = 576
+MIX = 16
 
 
 def kernel(
-    tok, wqkv, wout, nbr, out,
-    src, win, keys, vals, quer, att, mix, wqkv_v, wout_v, nb_v, nb_s,
+    tok, wqkv, nbr, out,
+    src, win, keys, vals, quer, att, wqkv_v, nb_v, nb_s,
+    score_a, score_b, prob_a, prob_b, share_a, share_b,
     load_sem, in_send, in_recv, halo_send, halo_recv, nb_send, nb_recv, nb_load, out_send, out_recv,
 ):
+    scores, probs, shares = (score_a, score_b), (prob_a, prob_b), (share_a, share_b)
     row, col = lax.axis_index("rows"), lax.axis_index("cols")
     y, x_lo, core = row // 4, (row // 2) % 2, row % 2
     x_hi, z = col // 4, col % 4
@@ -35,11 +40,9 @@
 
     loads = [pltpu.make_async_copy(tok.at[r], src.at[pl.ds(1, GROUPS), r], load_sem.at[r]) for r in range(2)]
     wload = pltpu.make_async_copy(wqkv, wqkv_v, load_sem.at[2])
-    oload = pltpu.make_async_copy(wout, wout_v, load_sem.at[3])
     for load in loads:
         load.start()
     wload.start()
-    oload.start()
 
     barrier = pltpu.get_barrier_semaphore()
     place = 8 * (row % 4) + col
@@ -59,6 +62,8 @@
             barrier, inc=1, device_id=(4 * (y + step_y) + 2 * x_lo + 1 - core, col), device_id_type=MESH
         )
 
+    prob_b[...] = jnp.zeros_like(prob_b)
+    share_b[...] = jnp.zeros_like(share_b)
     src[0] = jnp.zeros((2, 8, D), BF16)
     src[GROUPS + 1] = jnp.zeros((2, 8, D), BF16)
 
@@ -215,12 +220,14 @@
         def tile(n, carry):
             at = pl.multiple_of(n * 512, 512)
             qq = jnp.dot(x_in, wqkv_v[:, pl.ds(at, 512)], preferred_element_type=F32)
-            quer[:, pl.ds(at, 512)] = (qq.astype(BF16) * SCALE).astype(BF16)
+            quer[j, :, pl.ds(at, 512)] = (qq.astype(BF16) * SCALE).astype(BF16)
             return carry
 
         lax.fori_loop(0, 2, tile, 0)
 
     lane_head = lax.broadcasted_iota(jnp.int32, (1, QUAD), 1) // HEAD_DIM
+
+    key_at = lax.broadcasted_iota(jnp.int32, (1, KEYS), 1) // 64
 
     def attend(j, between):
         at_col = j
@@ -229,60 +236,82 @@
         if j == 3:
             at_col = j - jnp.where(t == 15, 1, 0)
 
-        def block(i, carry):
-            if between is not None:
-                pl.when(i == 2)(between)
+        def key_rows(i):
             at_blk = i + jnp.where(jnp.logical_and(g == 0, i == 0), 1, 0)
             at_blk = at_blk - jnp.where(jnp.logical_and(g == TILES - 1, i == 3), 1, 0)
-            rows = pl.ds(pl.multiple_of(64 * at_blk, 64), 192)
-            q_rows = pl.ds(pl.multiple_of(64 * i, 64), 64)
-            key_at = lax.broadcasted_iota(jnp.int32, (1, 576), 1) // 64
-            bias = jnp.zeros((1, 576), F32)
+            return pl.ds(pl.multiple_of(64 * at_blk, 64), 192)
+
+        def score(i, h):
+            rows, lanes = key_rows(i), pl.ds(h * QUAD, QUAD)
+            q4 = quer[j, pl.ds(pl.multiple_of(64 * i, 64), 64), lanes]
+            stacked = jnp.concatenate(
+                [jnp.where(lane_head == n, q4, jnp.zeros_like(q4)) for n in range(4)], axis=0
+            )
+            k4 = jnp.concatenate([keys[at_col + kc, rows, lanes] for kc in range(3)], axis=0)
+            scores[h % 2][...] = lax.dot_general(
+                stacked, k4, (((1,), (1,)), ((), ())), preferred_element_type=F32
+            )
+
+        def soften(bias, h):
+            for r in range(0, QUAD, 32):
+                s = scores[h % 2][r : r + 32, :] + bias
+                p = jnp.exp(s - jnp.max(s, axis=1, keepdims=True))
+                probs[h % 2][r : r + 32, :] = p.astype(BF16)
+                share = 1.0 / jnp.sum(p, axis=1, keepdims=True)
+                shares[h % 2][r : r + 32, :] = jnp.broadcast_to(share, (32, 128))
+
+        def gather(i, h):
+            rows, lanes = key_rows(i), pl.ds(h * QUAD, QUAD)
+            v4 = jnp.concatenate([vals[at_col + kc, rows, lanes] for kc in range(3)], axis=0)
+            r = jnp.dot(probs[h % 2][...], v4, preferred_element_type=F32)
+            share = shares[h % 2][...]
+            r = r * jnp.concatenate([share, share], axis=1)
+            o = jnp.where(lane_head == 0, r[0:64], r[64:128])
+            o = jnp.where(lane_head == 2, r[128:192], o)
+            o = jnp.where(lane_head == 3, r[192:256], o)
+            att[j, pl.ds(pl.multiple_of(64 * i, 64), 64), lanes] = o.astype(BF16)
+
+        def block(n, carry):
+            if between is not None:
+                pl.when(n == 2)(between)
+            i, before, after = turned(n), turned(jnp.maximum(n - 1, 0)), turned(jnp.minimum(n + 1, 3))
+            bias = jnp.zeros((1, KEYS), F32)
             for kc in range(3):
                 for kr in range(3):
                     entry = nb_s[i // 2, i % 2, 4 * (col % 2) + j, 3 * kr + kc]
                     here = jnp.where(entry >= 0, 0.0, -jnp.inf).astype(F32)
                     bias = jnp.where(key_at == 3 * kc + kr, here, bias)
-            for h in range(HEADS // 4):
-                lanes = pl.ds(h * QUAD, QUAD)
-                q4 = quer[q_rows, lanes]
-                stacked = jnp.concatenate(
-                    [jnp.where(lane_head == n, q4, jnp.zeros_like(q4)) for n in range(4)], axis=0
-                )
-                k4 = jnp.concatenate([keys[at_col + kc, rows, lanes] for kc in range(3)], axis=0)
-                v4 = jnp.concatenate([vals[at_col + kc, rows, lanes] for kc in range(3)], axis=0)
-                s = lax.dot_general(stacked, k4, (((1,), (1,)), ((), ())), preferred_element_type=F32)
-                s = s + bias
-                p = jnp.exp(s - jnp.max(s, axis=1, keepdims=True))
-                total = jnp.sum(p, axis=1, keepdims=True)
-                r = jnp.dot(p.astype(BF16), v4, preferred_element_type=F32) / total
-                o = jnp.where(lane_head == 0, r[0:64], r[64:128])
-                o = jnp.where(lane_head == 2, r[128:192], o)
-                o = jnp.where(lane_head == 3, r[192:256], o)
-                att[q_rows, lanes] = o.astype(BF16)
+            for h in range(QUADS):
+                if h < QUADS - 1:
+                    score(i, h + 1)
+                else:
+                    score(after, 0)
+                if h > 0:
+                    gather(i, h - 1)
+                else:
+                    gather(before, QUADS - 1)
+                soften(bias, h)
+
+            @pl.when(n > 0)
+            def _():
+                send_out(j, before)
+
             return carry
 
+        score(turned(0), 0)
         lax.fori_loop(0, 4, block, 0)
-
-        def tile(n, carry):
-            at = pl.multiple_of(n * 512, 512)
-            mm = jnp.dot(att[...], wout_v[:, pl.ds(at, 512)], preferred_element_type=F32).astype(BF16)
-            mix[j, :, :, pl.ds(at, 512)] = mm.reshape(32, 8, 512)
-            return carry
-
-        lax.fori_loop(0, 2, tile, 0)
-
-    def send_out(j):
+        gather(turned(3), QUADS - 1)
+        send_out(j, turned(3))
+
+    def turned(n):
+        return (n + 2 * core + x_hi) % 4
+
+    def send_out(j, i):
         def send(s, carry):
-            turn = (5 * s) % 16
-            z2 = (z + turn) % 4
-            x_hi2 = (x_hi + turn // 8) % 2
-            core2 = (core + turn // 4) % 2
-            col2 = 4 * x_hi2 + z2
-            pair = 8 * core2 + col2
-            source = mix.at[j, pl.ds(2 * pair, 2)]
+            z2 = (z + s) % 4
+            source = att.at[j, pl.ds(pl.multiple_of(64 * i + 16 * z2, 16), 16)]
             target = out.at[4 * t + j]
-            own = jnp.logical_and(s == 0, meets)
+            own = jnp.logical_and(jnp.logical_and(s == 0, meets), i == 2 * core + x_hi)
 
             @pl.when(own)
             def _():
@@ -292,12 +321,12 @@
             def _():
                 pltpu.make_async_remote_copy(
                     source, target, out_send, out_recv,
-                    device_id=(4 * y + 2 * core + core2, col2), device_id_type=MESH,
+                    device_id=(4 * y + 2 * core + i // 2, 4 * (i % 2) + z2), device_id_type=MESH,
                 ).start()
 
             return carry
 
-        lax.fori_loop(0, 16, send, 0)
+        lax.fori_loop(0, 4, send, 0)
 
     def lists_in():
         for b in range(2):
@@ -308,22 +337,27 @@
         down.wait()
 
     wload.wait()
-    oload.wait()
-    for k in range(3):
-        arrive(k)
-        project_inner(k)
+    arrive(0)
+    project_inner(0)
+    arrive(1)
+    project_inner(1)
     project_queries(0)
+    halo_wait(0)
+    project_halo((0,))
     lists_in()
-    for k in range(3):
-        halo_wait(k)
-    project_halo(range(3))
+    arrive(2)
+    project_inner(2)
+    project_queries(1)
+    halo_wait(1)
+    halo_wait(2)
+    project_halo((1, 2))
     for j in range(COLS):
         if j > 0:
-            project_queries(j)
+            if j > 1:
+                project_queries(j)
             halo_wait(j + 2)
             project_whole(j + 2)
         attend(j, functools.partial(arrive, j + 3) if j + 3 < STAGES else None)
-        send_out(j)
 
     for e in range(2):
         there = 2 * col + e
@@ -339,8 +373,8 @@
         def _(number=number):
             sent = win.at[:, pl.ds(0, 2 * number)]
             pltpu.make_async_copy(sent, sent, in_send).wait()
-            mixed = mix.at[:, pl.ds(0, 2 * number)]
-            pltpu.make_async_copy(mixed, mixed, out_send).wait()
+            back = att.at[:, pl.ds(0, 16 * number)]
+            pltpu.make_async_copy(back, back, out_send).wait()
 
     for k in range(STAGES):
 
@@ -355,27 +389,38 @@
     pltpu.make_async_copy(out, out, out_recv).wait()
 
 
+def mix_kernel(att, wout, out):
+    mm = jnp.dot(att[...].reshape(16 * MIX, D), wout[...], preferred_element_type=F32).astype(BF16)
+    mm = mm.reshape(MIX, 2, 8, D)
+    for r in range(2):
+        out[r] = mm[:, r]
+
+
 def per_device(tokens, qkv_weight, out_weight, neighbours):
     any_space = pl.BlockSpec(memory_space=pl.ANY)
     dma = pltpu.SemaphoreType.DMA
-    mixed = pl.pallas_call(
+    attended = pl.pallas_call(
         kernel,
-        out_shape=jax.ShapeDtypeStruct((GROUPS, 2, 8, D), BF16),
-        in_specs=[any_space] * 4,
+        out_shape=jax.ShapeDtypeStruct((GROUPS, 16, D), BF16),
+        in_specs=[any_space] * 3,
         out_specs=any_space,
         scratch_shapes=[
             pltpu.VMEM((GROUPS + 2, 2, 8, D), BF16),
             pltpu.VMEM((6, 48, 8, D), BF16),
             pltpu.VMEM((6, 384, D), BF16),
             pltpu.VMEM((6, 384, D), BF16),
-            pltpu.VMEM((256, D), BF16),
-            pltpu.VMEM((256, D), BF16),
-            pltpu.VMEM((4, 32, 8, D), BF16),
+            pltpu.VMEM((4, 256, D), BF16),
+            pltpu.VMEM((4, 256, D), BF16),
             pltpu.VMEM((D, 3 * D), BF16),
-            pltpu.VMEM((D, D), BF16),
             pltpu.VMEM((2, 2, 8, 9), jnp.int32),
             pltpu.SMEM((2, 2, 8, 9), jnp.int32),
-            dma((4,)),
+            pltpu.VMEM((QUAD, KEYS), F32),
+            pltpu.VMEM((QUAD, KEYS), F32),
+            pltpu.VMEM((QUAD, KEYS), BF16),
+            pltpu.VMEM((QUAD, KEYS), BF16),
+            pltpu.VMEM((QUAD, 128), F32),
+            pltpu.VMEM((QUAD, 128), F32),
+            dma((3,)),
             dma,
             dma((STAGES, 4)),
             dma((STAGES, 2)),
@@ -389,8 +434,19 @@
         compiler_params=pltpu.CompilerParams(
             collective_id=0, has_side_effects=True, vmem_limit_bytes=56 * 1024 * 1024
         ),
-    )(tokens.reshape(2, GROUPS, 8, D), qkv_weight, out_weight, neighbours)
-    return mixed.transpose(1, 0, 2, 3).reshape(1024, D)
+    )(tokens.reshape(2, GROUPS, 8, D), qkv_weight, neighbours)
+    mixed = pl.pallas_call(
+        mix_kernel,
+        out_shape=jax.ShapeDtypeStruct((2, GROUPS, 8, D), BF16),
+        grid=(GROUPS // MIX,),
+        in_specs=[
+            pl.BlockSpec((MIX, 16, D), lambda n: (n, 0, 0)),
+            pl.BlockSpec((D, D), lambda n: (0, 0)),
+        ],
+        out_specs=pl.BlockSpec((2, MIX, 8, D), lambda n: (0, n, 0, 0)),
+        compiler_params=pltpu.CompilerParams(vmem_limit_bytes=32 * 1024 * 1024),
+    )(attended, out_weight)
+    return mixed.reshape(1024, D)
 
 
 def solution(mesh):

time: 84.1 us -> 78.5 us (0.933)
  Pallas kernels: 80.4 us -> 76.5 us
  local copies, waits for them, and re-layouts: 3.12 us -> 1.59 us
    pallas_call x1 -> x2, Pallas kernels: 80.4 us -> 76.5 us  [the longest x1 72.8 us: per_device(): pl.pallas_call(kernel, out_shape=jax.ShapeDtypeStruct((GROUPS, 16, D), BF...]
    transpose x1 -> x0, local copies, waits for them, and re-layouts: 3.12 us -> none  [per_device(): return mixed.transpose(1, 0, 2, 3).reshape(1024, D)]
    unnamed x0 -> x4, local copies, waits for them, and re-layouts: none -> 1.59 us
where the time goes in v3:
time: 78.5 us; the launch traced here: 78.1 us
  Pallas kernels  76.5 us (97%)
  local copies, waits for them, and re-layouts  1.59 us (2%)
    pallas_call x1, Pallas kernels, per_device(): pl.pallas_call(kernel, out_shape=jax.ShapeDtypeStruct((GROUPS, 16, D), BF...  72.8 us
    pallas_call x1, Pallas kernels, per_device(): pl.pallas_call(mix_kernel, out_shape=jax.ShapeDtypeStruct((2, GROUPS, 8,...  3.73 us
    unnamed x4, local copies, waits for them, and re-layouts  1.59 us

profile of v3, /device:TPU:6, one launch (start us, length us, event | category | flops | bytes accessed | tf_op | source)
XLA Modules:
  0.0 78.1 jit_solution(12228469706312978239)
XLA Ops:
  0.0 0.0 copy-start.1
  0.0 72.8 %shard_map.46.att = bf16[64,16,1024]{2,1,0:T(8,128)(2,1)} custom-call(bf16[2,64,8,1024]{3,2,1,0:T(8,128)(2,1)} %bitcast.2, bf16[1024,3072]{1,0:T(8,128)(2,1)} %wqkv.1, s32[2,8,9]{2,1,0:T(8,128)} %nbr.1), custom_call_target="tpu_custom_call" | custom-call | tf_op jit(solution)/shard_map/pallas_call | solution.py:402
  72.8 0.0 copy-done.1
  72.8 0.0 copy-start
  72.8 1.6 %copy-done = bf16[64,16,1024]{2,1,0:T(8,128)(2,1)S(1)} copy-done((bf16[64,16,1024]{2,1,0:T(8,128)(2,1)S(1)}, bf16[64,16,1024]{2,1,0:T(8,128)(2,1)}, u32[]{:S(2)}) %copy-start) | copy-done | bytes 2097176
  74.4 3.7 %shard_map.47 = bf16[2,64,8,1024]{3,2,1,0:T(8,128)(2,1)} custom-call(bf16[64,16,1024]{2,1,0:T(8,128)(2,1)S(1)} %copy-done, bf16[1024,1024]{1,0:T(8,128)(2,1)S(1)} %copy-done.1), custom_call_target="tpu_custom_call" | custom-call | tf_op jit(solution)/shard_map/pallas_call | solution.py:438
Async XLA Ops:
  0.0 72.8 %copy-start.1 = (bf16[1024,1024]{1,0:T(8,128)(2,1)S(1)}, bf16[1024,1024]{1,0:T(8,128)(2,1)}, u32[]{:S(2)}) copy-start(bf16[1024,1024]{1,0:T(8,128)(2,1)} %wout.1) | copy-start | bytes 6291460
  72.8 1.6 %copy-start = (bf16[64,16,1024]{2,1,0:T(8,128)(2,1)S(1)}, bf16[64,16,1024]{2,1,0:T(8,128)(2,1)}, u32[]{:S(2)}) copy-start(bf16[64,16,1024]{2,1,0:T(8,128)(2,1)} %shard_map.46.att) | copy-start | bytes 6291460

commit v4 on v3

--- a/solution.py
+++ b/solution.py
@@ -172,14 +172,9 @@
             halo(k, False).wait_recv()
 
     def project(x_in, store):
-        def tile(n, carry):
-            at = pl.multiple_of(n * 512, 512)
-            kk = jnp.dot(x_in, wqkv_v[:, pl.ds(D + at, 512)], preferred_element_type=F32)
-            vv = jnp.dot(x_in, wqkv_v[:, pl.ds(2 * D + at, 512)], preferred_element_type=F32)
-            store(pl.ds(at, 512), kk.astype(BF16), vv.astype(BF16))
-            return carry
-
-        lax.fori_loop(0, 2, tile, 0)
+        kk = jnp.dot(x_in, wqkv_v[:, D : 2 * D], preferred_element_type=F32)
+        vv = jnp.dot(x_in, wqkv_v[:, 2 * D :], preferred_element_type=F32)
+        store(slice(None), kk.astype(BF16), vv.astype(BF16))
 
     def project_inner(k):
         c = place_of(k)
@@ -217,13 +212,8 @@
     def project_queries(j):
         x_in = win[j + 1, 8:40].reshape(256, D)
 
-        def tile(n, carry):
-            at = pl.multiple_of(n * 512, 512)
-            qq = jnp.dot(x_in, wqkv_v[:, pl.ds(at, 512)], preferred_element_type=F32)
-            quer[j, :, pl.ds(at, 512)] = (qq.astype(BF16) * SCALE).astype(BF16)
-            return carry
-
-        lax.fori_loop(0, 2, tile, 0)
+        qq = jnp.dot(x_in, wqkv_v[:, :D], preferred_element_type=F32)
+        quer[j] = (qq.astype(BF16) * SCALE).astype(BF16)
 
     lane_head = lax.broadcasted_iota(jnp.int32, (1, QUAD), 1) // HEAD_DIM
 
@@ -389,11 +379,19 @@
     pltpu.make_async_copy(out, out, out_recv).wait()
 
 
-def mix_kernel(att, wout, out):
-    mm = jnp.dot(att[...].reshape(16 * MIX, D), wout[...], preferred_element_type=F32).astype(BF16)
-    mm = mm.reshape(MIX, 2, 8, D)
-    for r in range(2):
-        out[r] = mm[:, r]
+def mix_kernel(att, wout, out, mixed, out_sem):
+    parts = GROUPS // MIX
+    at = lambda n: pl.ds(n * MIX, MIX)
+    stores = [pltpu.make_async_copy(mixed.at[n], out.at[:, at(n)], out_sem.at[n]) for n in range(parts)]
+    for n in range(parts):
+        x_in = att[at(n)].reshape(16 * MIX, D)
+        mm = jnp.dot(x_in, wout[...], preferred_element_type=F32).astype(BF16)
+        mm = mm.reshape(MIX, 2, 8, D)
+        for r in range(2):
+            mixed[n, r] = mm[:, r]
+        stores[n].start()
+    for store in stores:
+        store.wait()
 
 
 def per_device(tokens, qkv_weight, out_weight, neighbours):
@@ -438,12 +436,12 @@
     mixed = pl.pallas_call(
         mix_kernel,
         out_shape=jax.ShapeDtypeStruct((2, GROUPS, 8, D), BF16),
-        grid=(GROUPS // MIX,),
-        in_specs=[
-            pl.BlockSpec((MIX, 16, D), lambda n: (n, 0, 0)),
-            pl.BlockSpec((D, D), lambda n: (0, 0)),
+        in_specs=[pl.BlockSpec(memory_space=pltpu.VMEM)] * 2,
+        out_specs=pl.BlockSpec(memory_space=pltpu.HBM),
+        scratch_shapes=[
+            pltpu.VMEM((GROUPS // MIX, 2, MIX, 8, D), BF16),
+            dma((GROUPS // MIX,)),
         ],
-        out_specs=pl.BlockSpec((2, MIX, 8, D), lambda n: (0, n, 0, 0)),
         compiler_params=pltpu.CompilerParams(vmem_limit_bytes=32 * 1024 * 1024),
     )(attended, out_weight)
     return mixed.reshape(1024, D)

time: 78.5 us -> 76.8 us (0.978)
  Pallas kernels: 76.5 us -> 74.6 us
    pallas_call x1, Pallas kernels: 72.8 us -> 71.4 us  [per_device(): pl.pallas_call(kernel, out_shape=jax.ShapeDtypeStruct((GROUPS, 16, D), BF...]
where the time goes in v4:
time: 76.8 us; the launch traced here: 76.4 us
  Pallas kernels  74.6 us (97%)
  local copies, waits for them, and re-layouts  1.59 us (2%)
    pallas_call x1, Pallas kernels, per_device(): pl.pallas_call(kernel, out_shape=jax.ShapeDtypeStruct((GROUPS, 16, D), BF...  71.4 us
    pallas_call x1, Pallas kernels, per_device(): pl.pallas_call(mix_kernel, out_shape=jax.ShapeDtypeStruct((2, GROUPS, 8,...  3.16 us
    unnamed x4, local copies, waits for them, and re-layouts  1.59 us

profile of v4, /device:TPU:6, one launch (start us, length us, event | category | flops | bytes accessed | tf_op | source)
XLA Modules:
  0.0 76.4 jit_solution(918614661139430639)
XLA Ops:
  0.0 0.0 copy-start.1
  0.0 71.4 %shard_map.46.att = bf16[64,16,1024]{2,1,0:T(8,128)(2,1)} custom-call(bf16[2,64,8,1024]{3,2,1,0:T(8,128)(2,1)} %bitcast.2, bf16[1024,3072]{1,0:T(8,128)(2,1)} %wqkv.1, s32[2,8,9]{2,1,0:T(8,128)} %nbr.1), custom_call_target="tpu_custom_call" | custom-call | tf_op jit(solution)/shard_map/pallas_call | solution.py:400
  71.5 0.0 copy-done.1
  71.5 0.0 copy-start
  71.5 1.6 %copy-done = bf16[64,16,1024]{2,1,0:T(8,128)(2,1)S(1)} copy-done((bf16[64,16,1024]{2,1,0:T(8,128)(2,1)S(1)}, bf16[64,16,1024]{2,1,0:T(8,128)(2,1)}, u32[]{:S(2)}) %copy-start) | copy-done | bytes 2097176
  73.1 3.2 %shard_map.47 = bf16[2,64,8,1024]{3,2,1,0:T(8,128)(2,1)} custom-call(bf16[64,16,1024]{2,1,0:T(8,128)(2,1)S(1)} %copy-done, bf16[1024,1024]{1,0:T(8,128)(2,1)S(1)} %copy-done.1), custom_call_target="tpu_custom_call" | custom-call | tf_op jit(solution)/shard_map/pallas_call | solution.py:436
Async XLA Ops:
  0.0 71.5 %copy-start.1 = (bf16[1024,1024]{1,0:T(8,128)(2,1)S(1)}, bf16[1024,1024]{1,0:T(8,128)(2,1)}, u32[]{:S(2)}) copy-start(bf16[1024,1024]{1,0:T(8,128)(2,1)} %wout.1) | copy-start | bytes 6291460
  71.5 1.6 %copy-start = (bf16[64,16,1024]{2,1,0:T(8,128)(2,1)S(1)}, bf16[64,16,1024]{2,1,0:T(8,128)(2,1)}, u32[]{:S(2)}) copy-start(bf16[64,16,1024]{2,1,0:T(8,128)(2,1)} %shard_map.46.att) | copy-start | bytes 6291460

commit v5 on v4

--- a/solution.py
+++ b/solution.py
@@ -45,14 +45,21 @@
     wload.start()
 
     barrier = pltpu.get_barrier_semaphore()
-    place = 8 * (row % 4) + col
+    meets = core == x_lo
 
     def greet(i, carry):
-        other = (place + i) % 32
-        pl.semaphore_signal(barrier, inc=1, device_id=(4 * y + other // 8, other % 8), device_id_type=MESH)
+        turn = i // 8
+        other = jnp.where(turn == 0, x_lo, jnp.where(turn == 1, 2 + x_lo, 2 * core + 1 - x_lo))
+        col2 = (col + i) % 8
+        itself = jnp.logical_and(other == 2 * x_lo + core, col2 == col)
+
+        @pl.when(jnp.logical_not(itself))
+        def _():
+            pl.semaphore_signal(barrier, inc=1, device_id=(4 * y + other, col2), device_id_type=MESH)
+
         return carry
 
-    lax.fori_loop(1, 32, greet, 0)
+    lax.fori_loop(0, 24, greet, 0)
     step_y = 2 * core - 1
     outer = jnp.logical_and(y + step_y >= 0, y + step_y < TILES // 2)
 
@@ -79,7 +86,7 @@
 
     for load in loads:
         load.wait()
-    pl.semaphore_wait(barrier, jnp.where(outer, 32, 31))
+    pl.semaphore_wait(barrier, 24 - jnp.where(meets, 1, 0) + jnp.where(outer, 1, 0))
 
     for e in range(2):
         there = 2 * col + e
@@ -98,7 +105,6 @@
 
     at_row = 8 + 16 * core + 2 * col
     band = 2 * core + x_hi
-    meets = core == x_lo
 
     shift = jnp.where(t == 0, 1, 0)
 

time: 76.8 us -> 76.2 us (level)
  no operation moved by 1% of the time
where the time goes in v5:
time: 76.2 us; the launch traced here: 76.1 us
  Pallas kernels  74.3 us (98%)
  local copies, waits for them, and re-layouts  1.59 us (2%)
    pallas_call x1, Pallas kernels, per_device(): pl.pallas_call(kernel, out_shape=jax.ShapeDtypeStruct((GROUPS, 16, D), BF...  71.2 us
    pallas_call x1, Pallas kernels, per_device(): pl.pallas_call(mix_kernel, out_shape=jax.ShapeDtypeStruct((2, GROUPS, 8,...  3.16 us
    unnamed x4, local copies, waits for them, and re-layouts  1.59 us

profile of v5, /device:TPU:6, one launch (start us, length us, event | category | flops | bytes accessed | tf_op | source)
XLA Modules:
  0.0 76.1 jit_solution(7363124802786045466)
XLA Ops:
  0.0 0.0 copy-start.1
  0.0 71.2 %shard_map.46.att = bf16[64,16,1024]{2,1,0:T(8,128)(2,1)} custom-call(bf16[2,64,8,1024]{3,2,1,0:T(8,128)(2,1)} %bitcast.2, bf16[1024,3072]{1,0:T(8,128)(2,1)} %wqkv.1, s32[2,8,9]{2,1,0:T(8,128)} %nbr.1), custom_call_target="tpu_custom_call" | custom-call | tf_op jit(solution)/shard_map/pallas_call | solution.py:406
  71.2 0.0 copy-done.1
  71.2 0.0 copy-start
  71.2 1.6 %copy-done = bf16[64,16,1024]{2,1,0:T(8,128)(2,1)S(1)} copy-done((bf16[64,16,1024]{2,1,0:T(8,128)(2,1)S(1)}, bf16[64,16,1024]{2,1,0:T(8,128)(2,1)}, u32[]{:S(2)}) %copy-start) | copy-done | bytes 2097176
  72.8 3.2 %shard_map.47 = bf16[2,64,8,1024]{3,2,1,0:T(8,128)(2,1)} custom-call(bf16[64,16,1024]{2,1,0:T(8,128)(2,1)S(1)} %copy-done, bf16[1024,1024]{1,0:T(8,128)(2,1)S(1)} %copy-done.1), custom_call_target="tpu_custom_call" | custom-call | tf_op jit(solution)/shard_map/pallas_call | solution.py:442
Async XLA Ops:
  0.0 71.2 %copy-start.1 = (bf16[1024,1024]{1,0:T(8,128)(2,1)S(1)}, bf16[1024,1024]{1,0:T(8,128)(2,1)}, u32[]{:S(2)}) copy-start(bf16[1024,1024]{1,0:T(8,128)(2,1)} %wout.1) | copy-start | bytes 6291460
  71.2 1.6 %copy-start = (bf16[64,16,1024]{2,1,0:T(8,128)(2,1)S(1)}, bf16[64,16,1024]{2,1,0:T(8,128)(2,1)}, u32[]{:S(2)}) copy-start(bf16[64,16,1024]{2,1,0:T(8,128)(2,1)} %shard_map.46.att) | copy-start | bytes 6291460

commit v6 on v5

--- a/solution.py
+++ b/solution.py
@@ -88,21 +88,6 @@
         load.wait()
     pl.semaphore_wait(barrier, 24 - jnp.where(meets, 1, 0) + jnp.where(outer, 1, 0))
 
-    for e in range(2):
-        there = 2 * col + e
-        dest = (4 * y + 2 * x_hi + x_lo, there % 8)
-        own = jnp.logical_and(dest[0] == row, dest[1] == col)
-
-        @pl.when(own)
-        def _(dest=dest):
-            pltpu.make_async_copy(nbr, nb_v.at[core], nb_recv.at[core]).start()
-
-        @pl.when(jnp.logical_not(own))
-        def _(dest=dest, e=e):
-            pltpu.make_async_remote_copy(
-                nbr, nb_v.at[core], nb_send.at[e], nb_recv.at[core], device_id=dest, device_id_type=MESH
-            ).start()
-
     at_row = 8 + 16 * core + 2 * col
     band = 2 * core + x_hi
 
@@ -135,7 +120,24 @@
 
         return carry
 
-    lax.fori_loop(0, 16 * STAGES, send_in, 0)
+    lax.fori_loop(0, 16, send_in, 0)
+
+    for e in range(2):
+        there = 2 * col + e
+        dest = (4 * y + 2 * x_hi + x_lo, there % 8)
+        own = jnp.logical_and(dest[0] == row, dest[1] == col)
+
+        @pl.when(own)
+        def _(dest=dest):
+            pltpu.make_async_copy(nbr, nb_v.at[core], nb_recv.at[core]).start()
+
+        @pl.when(jnp.logical_not(own))
+        def _(dest=dest, e=e):
+            pltpu.make_async_remote_copy(
+                nbr, nb_v.at[core], nb_send.at[e], nb_recv.at[core], device_id=dest, device_id_type=MESH
+            ).start()
+
+    lax.fori_loop(16, 16 * STAGES, send_in, 0)
 
     def band_wait(k, b):
         part = win.at[0, pl.ds(8 + 8 * b, 8)]

time: 76.2 us -> 76.3 us (level)
  no operation moved by 1% of the time
where the time goes in v6:
time: 76.3 us; the launch traced here: 76.2 us
  Pallas kernels  74.4 us (98%)
  local copies, waits for them, and re-layouts  1.59 us (2%)
    pallas_call x1, Pallas kernels, per_device(): pl.pallas_call(kernel, out_shape=jax.ShapeDtypeStruct((GROUPS, 16, D), BF...  71.3 us
    pallas_call x1, Pallas kernels, per_device(): pl.pallas_call(mix_kernel, out_shape=jax.ShapeDtypeStruct((2, GROUPS, 8,...  3.16 us
    unnamed x4, local copies, waits for them, and re-layouts  1.59 us

profile of v6, /device:TPU:6, one launch (start us, length us, event | category | flops | bytes accessed | tf_op | source)
XLA Modules:
  0.0 76.2 jit_solution(12821972678640921262)
XLA Ops:
  0.0 0.0 copy-start.1
  0.0 71.3 %shard_map.46.att = bf16[64,16,1024]{2,1,0:T(8,128)(2,1)} custom-call(bf16[2,64,8,1024]{3,2,1,0:T(8,128)(2,1)} %bitcast.2, bf16[1024,3072]{1,0:T(8,128)(2,1)} %wqkv.1, s32[2,8,9]{2,1,0:T(8,128)} %nbr.1), custom_call_target="tpu_custom_call" | custom-call | tf_op jit(solution)/shard_map/pallas_call | solution.py:408
  71.3 0.0 copy-done.1
  71.3 0.0 copy-start
  71.3 1.6 %copy-done = bf16[64,16,1024]{2,1,0:T(8,128)(2,1)S(1)} copy-done((bf16[64,16,1024]{2,1,0:T(8,128)(2,1)S(1)}, bf16[64,16,1024]{2,1,0:T(8,128)(2,1)}, u32[]{:S(2)}) %copy-start) | copy-done | bytes 2097176
  72.9 3.2 %shard_map.47 = bf16[2,64,8,1024]{3,2,1,0:T(8,128)(2,1)} custom-call(bf16[64,16,1024]{2,1,0:T(8,128)(2,1)S(1)} %copy-done, bf16[1024,1024]{1,0:T(8,128)(2,1)S(1)} %copy-done.1), custom_call_target="tpu_custom_call" | custom-call | tf_op jit(solution)/shard_map/pallas_call | solution.py:444
Async XLA Ops:
  0.0 71.3 %copy-start.1 = (bf16[1024,1024]{1,0:T(8,128)(2,1)S(1)}, bf16[1024,1024]{1,0:T(8,128)(2,1)}, u32[]{:S(2)}) copy-start(bf16[1024,1024]{1,0:T(8,128)(2,1)} %wout.1) | copy-start | bytes 6291460
  71.3 1.6 %copy-start = (bf16[64,16,1024]{2,1,0:T(8,128)(2,1)S(1)}, bf16[64,16,1024]{2,1,0:T(8,128)(2,1)}, u32[]{:S(2)}) copy-start(bf16[64,16,1024]{2,1,0:T(8,128)(2,1)} %shard_map.46.att) | copy-start | bytes 6291460
